TPU v7x, 32 devices: a whole 2x2x4 slice. The times are simulated.
32 devices in a mesh: shots: 2 (over x), gx: 8 (over z, y), gy: 2 (over core).
Axes of the slice: x: 2, y: 2, z: 4, core: 2. Of those that a mesh axis runs over, the one named last changes fastest.
Arguments:
- field_now: float32 [512, 96, 128], P(('shots', 'gx'), 'gy'), parts along dimension 0, may hold values from -6 to 6
- field_prev: float32 [512, 96, 128], P(('shots', 'gx'), 'gy'), parts along dimension 0, may hold values from -6 to 6
- courant_squared: float32 [256, 96, 128], P('gx', 'gy'), may hold values from 0.05 to 0.18, as said below
- source_cells: int32 [3, 16], P(None, 'shots'), parts along dimension 1, may hold values from 0 to 127, as said below
- source_wave: float32 [4, 16], P(None, 'shots'), parts along dimension 1, may hold values from -8 to 8
- receiver_cells: int32 [3, 512], P(None, 'shots'), parts along dimension 1, may hold values from 0 to 127, as said below
- receiver_wave: float32 [4, 512], P(None, 'shots'), parts along dimension 1, may hold values from -8 to 8
- snapshot_steps: int32 [4, 2], P('shots'), parts along dimension 0, may hold values from 1 to 4, as said below
- lag_offsets: int32 [17], replicated, may hold values from -8 to 8
Outputs:
- final_field: float32 [512, 96, 128], P(('shots', 'gx'), 'gy'), parts along dimension 0
- extended_image: float32 [256, 17, 1536], P(('shots', 'gx'), None, 'gy'), parts along dimension 0
There are 2 independent parts, one for each index of `shots`. A program takes and returns all parts, laid end to end along the dimension named above; an argument that names none is the same for every part. Nothing has to cross between parts.
Inputs may be any that keep to these rules, and one draw needn't show every extreme that they name: `courant_squared`: both fields' rows of the same model cell hold the same value. `source_cells`: row 0 is an x cell below 128, row 1 a y cell below 96, row 2 a z cell below 128. `receiver_cells`: row 0 is an x cell below 128, row 1 a y cell below 96, row 2 a z cell below 128. `snapshot_steps`: column 0 lies in 1 to 2, column 1 in 3 to 4.
All inputs are finite; a program needn't handle non-finite values.
Results may differ from a plain program's by a relative error of at most 0.0003.
Values sent between devices are 32-bit elements; how exact they have to be, the bound alone decides.
A program may use at most 64 MiB of HBM per device.

v0:
```python
import functools

import jax
import jax.numpy as jnp
from jax import lax
from jax.experimental import pallas as pl
from jax.experimental.pallas import tpu as pltpu
from jax.sharding import PartitionSpec as P

STEPS = 4
WIDTH = 4
GROUP = 4
ROW = 8
centre_weight = -205.0 / 72.0
stencil_weights = (1.6, -0.2, 8.0 / 315.0, -1.0 / 560.0)
MESH = pl.DeviceIdType.MESH
f32, bf16 = jnp.float32, jnp.bfloat16


def halves(value):
    high = value.astype(bf16)
    low = (value - high.astype(f32)).astype(bf16)
    return high, low


def kernel(
    now_ref, prev_ref, courant_ref, scell_ref, swave_ref, rcell_ref, rwave_ref, steps_ref, lag_ref,
    final_ref, image_ref,
    fields, courant, band, inject, choose_own, choose_other, snap, other, x_own, x_other, cells, waves,
    x_send, x_recv, y_send, y_recv, t_send, t_recv, local,
):
    nx, ny, nz = now_ref.shape
    lags = lag_ref.shape[0]
    points = cells.shape[1]
    loop = lax.axis_size("gx")
    half = loop // 2
    turn = loop // 4
    gx = lax.axis_index("gx")
    gy = lax.axis_index("gy")
    relative = lax.rem(gx - turn + loop, loop)
    which = relative // half
    slab = lax.rem(relative, half)
    low_id = {"gx": lax.rem(gx - 1 + loop, loop)}
    high_id = {"gx": lax.rem(gx + 1, loop)}
    peer_id = {"gy": 1 - gy}
    trade_id = {"gx": lax.rem(gx + half, loop)}
    has_low = slab > 0
    has_high = slab < half - 1
    y_src = pl.multiple_of(jnp.where(gy == 0, ny, ROW), ROW)
    y_src0 = pl.multiple_of(jnp.where(gy == 0, ny - ROW, 0), ROW)
    y_dst = pl.multiple_of(jnp.where(gy == 0, 0, ny + ROW), ROW)

    inner = (pl.ds(WIDTH, nx), pl.ds(ROW, ny))
    loads = [
        pltpu.make_async_copy(now_ref, fields.at[0, inner[0], inner[1]], local.at[0]),
        pltpu.make_async_copy(prev_ref, fields.at[1, inner[0], inner[1]], local.at[1]),
        pltpu.make_async_copy(courant_ref, courant, local.at[2]),
    ]
    for load in loads:
        load.start()

    for parity in range(2):
        edge = jnp.zeros((WIDTH, ny + 2 * ROW, nz), f32)
        fields[parity, 0:WIDTH] = edge
        fields[parity, WIDTH + nx:] = edge
        side = jnp.zeros((nx, ROW, nz), f32)
        fields[parity, WIDTH:WIDTH + nx, 0:ROW] = side
        fields[parity, WIDTH:WIDTH + nx, ROW + ny:] = side

    barrier = pltpu.get_barrier_semaphore()
    pl.semaphore_signal(barrier, inc=1, device_id=peer_id, device_id_type=MESH)
    pl.semaphore_signal(barrier, inc=1, device_id=trade_id, device_id_type=MESH)

    @pl.when(has_low)
    def _():
        pl.semaphore_signal(barrier, inc=1, device_id=low_id, device_id_type=MESH)

    @pl.when(has_high)
    def _():
        pl.semaphore_signal(barrier, inc=1, device_id=high_id, device_id_type=MESH)

    pl.semaphore_wait(barrier, 2 + has_low.astype(jnp.int32) + has_high.astype(jnp.int32))

    rows = pl.ds(ROW, ny)

    def x_copy(s, way):
        at = s % 2
        if s == 0:
            src = now_ref.at[pl.ds(0 if way == 0 else nx - WIDTH, WIDTH)]
        else:
            src = fields.at[at, pl.ds(WIDTH if way == 0 else nx, WIDTH), rows]
        return pltpu.make_async_remote_copy(
            src_ref=src,
            dst_ref=fields.at[at, pl.ds(WIDTH + nx if way == 0 else 0, WIDTH), rows],
            send_sem=x_send.at[s, way],
            recv_sem=x_recv.at[s, way],
            device_id=low_id if way == 0 else high_id,
            device_id_type=MESH,
        )

    parts = ((GROUP, nx - 2 * GROUP), (0, GROUP), (nx - GROUP, GROUP))

    def y_copy(s, part):
        at = s % 2
        begin, size = parts[part]
        if s == 0:
            src = now_ref.at[pl.ds(begin, size), pl.ds(y_src0, ROW)]
        else:
            src = fields.at[at, pl.ds(WIDTH + begin, size), pl.ds(y_src, ROW)]
        return pltpu.make_async_remote_copy(
            src_ref=src,
            dst_ref=fields.at[at, pl.ds(WIDTH + begin, size), pl.ds(y_dst, ROW)],
            send_sem=y_send.at[s, part],
            recv_sem=y_recv.at[s, part],
            device_id=peer_id,
            device_id_type=MESH,
        )

    def trade(k):
        return pltpu.make_async_remote_copy(
            src_ref=snap.at[k],
            dst_ref=other.at[k],
            send_sem=t_send.at[k],
            recv_sem=t_recv.at[k],
            device_id=trade_id,
            device_id_type=MESH,
        )

    def x_start(s):
        @pl.when(has_low)
        def _():
            x_copy(s, 0).start()

        @pl.when(has_high)
        def _():
            x_copy(s, 1).start()

    def x_arrived(s):
        @pl.when(has_high)
        def _():
            x_copy(s, 0).wait_recv()

        @pl.when(has_low)
        def _():
            x_copy(s, 1).wait_recv()

    def x_left(s):
        @pl.when(has_low)
        def _():
            x_copy(s, 0).wait_send()

        @pl.when(has_high)
        def _():
            x_copy(s, 1).wait_send()

    x_start(0)
    for part in range(3):
        y_copy(0, part).start()

    apart = jnp.abs(
        lax.broadcasted_iota(jnp.int32, (nz, nz), 0) - lax.broadcasted_iota(jnp.int32, (nz, nz), 1)
    )
    matrix = jnp.where(apart == 0, f32(3.0 * centre_weight), f32(0.0))
    for k, weight in enumerate(stencil_weights, 1):
        matrix = jnp.where(apart == k, f32(weight), matrix)
    matrix_high, matrix_low = halves(matrix)
    band[0:nz] = matrix_high
    band[nz:2 * nz] = matrix_high
    band[2 * nz:] = matrix_low

    is_source = which == 0
    count = scell_ref.shape[1]
    cells[...] = jnp.full(cells.shape, -1, jnp.int32)
    waves[...] = jnp.zeros(waves.shape, f32)
    cells[0:3, 0:count] = scell_ref[...]
    waves[0:STEPS, 0:count] = swave_ref[...]
    cell = jnp.where(is_source, cells[0:3], rcell_ref[...])
    wave = jnp.where(is_source, waves[0:STEPS], rwave_ref[...])
    at_x = cell[0:1] - slab * nx
    at_y = cell[1:2] - gy * ny
    inside = (at_x >= 0) & (at_x < nx) & (at_y >= 0) & (at_y < ny)
    line = jnp.where(inside, at_x * ny + at_y, -1)
    at_z = lax.broadcasted_iota(jnp.int32, (nz, points), 0) == cell[2:3]
    amounts = []
    for s in range(STEPS):
        high, low = halves(jnp.where(at_z, wave[s:s + 1], 0.0))
        amounts.append(jnp.concatenate([high, low], axis=1))
    amounts = jnp.concatenate(amounts, axis=0)
    chunk = GROUP * ny

    def spread(g, carry):
        row = lax.broadcasted_iota(jnp.int32, (chunk, points), 0) + g * chunk
        hit = jnp.where(row == line, f32(1.0), f32(0.0)).astype(bf16)
        hit = jnp.concatenate([hit, hit], axis=1)
        added = lax.dot_general(
            hit, amounts, (((1,), (1,)), ((), ())), preferred_element_type=f32
        )
        for s in range(STEPS):
            inject[s, pl.ds(pl.multiple_of(g * chunk, chunk), chunk), :] = added[:, s * nz:(s + 1) * nz]
        return carry

    lax.fori_loop(0, nx // GROUP, spread, 0)

    quarter = nz // 4
    lane = lax.broadcasted_iota(jnp.int32, (nz, nz), 1)
    depth = lax.broadcasted_iota(jnp.int32, (nz, nz), 0)
    twice = 2 * (which * quarter + lax.rem(lane, quarter)) - depth
    spot = lane // quarter
    sign = jnp.where(is_source, -1, 1)
    far = 4 * nz

    def choose(h, carry):
        lag = lag_ref[h] * sign
        for r in range(4):
            mine = jnp.where(spot == r, twice, far)
            choose_own[h, r * nz:(r + 1) * nz, :] = jnp.where(mine == -lag, f32(1.0), f32(0.0)).astype(bf16)
            choose_other[h, r * nz:(r + 1) * nz, :] = jnp.where(mine == lag, f32(1.0), f32(0.0)).astype(bf16)
        return carry

    lax.fori_loop(0, lags, choose, 0)

    for load in loads:
        load.wait()

    def group(s, g):
        a, b = (s - 1) % 2, s % 2
        base = WIDTH + g * GROUP
        centre = fields[a, pl.ds(base, GROUP), rows, :].reshape(GROUP * ny, nz)
        high, low = halves(centre)
        along = jnp.dot(
            jnp.concatenate([high, low, high], axis=1), band[...], preferred_element_type=f32
        )
        for i in range(GROUP):
            x = base + i
            total = along[i * ny:(i + 1) * ny]
            for k, weight in enumerate(stencil_weights, 1):
                pair = fields[a, x + k, rows, :] + fields[a, x - k, rows, :]
                pair = pair + fields[a, x, pl.ds(ROW + k, ny), :] + fields[a, x, pl.ds(ROW - k, ny), :]
                total = total + weight * pair
            at = g * GROUP + i
            fields[b, x, rows, :] = (
                2.0 * fields[a, x, rows, :]
                - fields[b, x, rows, :]
                + courant[at] * total
                + inject[s - 1, pl.ds(pl.multiple_of(at * ny, ny), ny), :]
            )

    def hold(k, wanted):
        def one(i, carry):
            for r in range(4):
                cut = pl.ds(ROW + 2 * r, ny // ROW, ROW)
                early = fields[1, WIDTH + 2 * i, cut, :]
                late = fields[0, WIDTH + 2 * i, cut, :]
                snap[k, r, pl.ds(i, ny // ROW, nx // 2), :] = jnp.where(wanted == 2 * k + 1, early, late)
            return carry

        lax.fori_loop(0, nx // 2, one, 0)

    def split(ref, k, to):
        count = ref.shape[2]
        for r in range(4):
            high, low = halves(ref[k, r])
            to[0:count, r * nz:(r + 1) * nz] = high
            to[count:, r * nz:(r + 1) * nz] = low

    def image(k):
        split(snap, k, x_own)
        trade(k).wait_recv()
        split(other, k, x_other)
        count = snap.shape[2]

        def one(h, carry):
            mine = jnp.dot(x_own[...], choose_own[h], preferred_element_type=f32)
            theirs = jnp.dot(x_other[...], choose_other[h], preferred_element_type=f32)
            value = (mine[:count] + mine[count:]) * (theirs[:count] + theirs[count:])
            place = pl.ds(h, count, image_ref.shape[0] // count)
            if k == 0:
                image_ref[place, :] = value
            else:
                image_ref[place, :] = image_ref[place, :] + value
            return carry

        lax.fori_loop(0, lags, one, 0)

    groups = nx // GROUP
    for s in range(1, STEPS + 1):
        y_copy(s - 1, 0).wait_recv()
        if s >= 2:
            x_left(s - 2)
            for part in range(3):
                y_copy(s - 2, part).wait_send()

        def inside_group(g, carry):
            group(s, g)
            return carry

        def rim_group(i, carry):
            group(s, i * (groups - 1))
            return carry

        lax.fori_loop(1, groups - 1, inside_group, 0)
        if s < STEPS:
            y_copy(s, 0).start()
        x_arrived(s - 1)
        y_copy(s - 1, 1).wait_recv()
        y_copy(s - 1, 2).wait_recv()
        lax.fori_loop(0, 2, rim_group, 0)
        if s < STEPS:
            x_start(s)
            y_copy(s, 1).start()
            y_copy(s, 2).start()
        if s % 2 == 0:
            k = s // 2 - 1
            hold(k, steps_ref[which, k])
            trade(k).start()
    store = pltpu.make_async_copy(fields.at[STEPS % 2, inner[0], inner[1]], final_ref, local.at[3])
    store.start()
    x_left(STEPS - 1)
    for part in range(3):
        y_copy(STEPS - 1, part).wait_send()
    image(0)
    image(1)
    trade(0).wait_send()
    trade(1).wait_send()
    store.wait()


def body(now, prev, courant, source_cells, source_wave, receiver_cells, receiver_wave, steps, lag_offsets):
    nx, ny, nz = now.shape
    lags = lag_offsets.shape[0]
    deep = -(-lags // 8) * 8
    packed = (nx // 2) * (ny // 8)
    points = receiver_cells.shape[1]
    vmem = pl.BlockSpec(memory_space=pltpu.VMEM)
    smem = pl.BlockSpec(memory_space=pltpu.SMEM)
    anywhere = pl.BlockSpec(memory_space=pl.ANY)
    dma = pltpu.SemaphoreType.DMA
    final, image = pl.pallas_call(
        kernel,
        out_shape=(
            jax.ShapeDtypeStruct(now.shape, f32),
            jax.ShapeDtypeStruct((packed * deep, nz), f32),
        ),
        in_specs=[anywhere] * 3 + [vmem] * 4 + [smem] * 2,
        out_specs=(anywhere, vmem),
        scratch_shapes=[
            pltpu.VMEM((2, nx + 2 * WIDTH, ny + 2 * ROW, nz), f32),
            pltpu.VMEM((nx, ny, nz), f32),
            pltpu.VMEM((3 * nz, nz), bf16),
            pltpu.VMEM((STEPS, nx * ny, nz), f32),
            pltpu.VMEM((lags, 4 * nz, nz), bf16),
            pltpu.VMEM((lags, 4 * nz, nz), bf16),
            pltpu.VMEM((2, 4, packed, nz), f32),
            pltpu.VMEM((2, 4, packed, nz), f32),
            pltpu.VMEM((2 * packed, 4 * nz), bf16),
            pltpu.VMEM((2 * packed, 4 * nz), bf16),
            pltpu.VMEM((8, points), jnp.int32),
            pltpu.VMEM((8, points), f32),
            dma((STEPS, 2)),
            dma((STEPS, 2)),
            dma((STEPS, 3)),
            dma((STEPS, 3)),
            dma((2,)),
            dma((2,)),
            dma((4,)),
        ],
        compiler_params=pltpu.CompilerParams(
            collective_id=0, has_side_effects=True, vmem_limit_bytes=48 * 1024 * 1024
        ),
    )(now, prev, courant, source_cells, source_wave, receiver_cells, receiver_wave, steps, lag_offsets)
    image = image.reshape(ny // 8, nx // 2, deep, nz)[:, :, :lags]
    image = jnp.transpose(image, (1, 2, 0, 3)).reshape(nx // 2, lags, (ny // 8) * nz)
    return final, image


def solution(mesh):
    placed = (
        P(("shots", "gx"), "gy", None),
        P(("shots", "gx"), "gy", None),
        P("gx", "gy", None),
        P(None, "shots"),
        P(None, "shots"),
        P(None, "shots"),
        P(None, "shots"),
        P("shots", None),
        P(),
    )
    return jax.shard_map(
        body,
        mesh=mesh,
        in_specs=placed,
        out_specs=(P(("shots", "gx"), "gy", None), P(("shots", "gx"), None, "gy")),
        check_vma=False,
    )
```

profile of v0, /device:TPU:0, one launch (start us, length us, event | category | flops | bytes accessed | tf_op | source)
XLA Modules:
  0.0 57.4 jit_solution(1768930154853024977)
XLA Ops:
  0.6 0.0 copy-start
  0.6 1.1 %copy-done = f32[32,48,128]{2,1,0:T(8,128)S(1)} copy-done((f32[32,48,128]{2,1,0:T(8,128)S(1)}, f32[32,48,128]{2,1,0:T(8,128)}, u32[]{:S(2)}) %copy-start) | copy-done | bytes 786456
  1.8 0.0 copy-start.1
  1.8 1.1 %copy-done.1 = f32[32,48,128]{2,1,0:T(8,128)S(1)} copy-done((f32[32,48,128]{2,1,0:T(8,128)S(1)}, f32[32,48,128]{2,1,0:T(8,128)}, u32[]{:S(2)}) %copy-start.1) | copy-done | bytes 786456
  2.9 0.0 copy-start.2
  2.9 1.1 %copy-done.2 = f32[32,48,128]{2,1,0:T(8,128)S(1)} copy-done((f32[32,48,128]{2,1,0:T(8,128)S(1)}, f32[32,48,128]{2,1,0:T(8,128)}, u32[]{:S(2)}) %copy-start.2) | copy-done | bytes 786456
  4.0 0.0 copy-start.3
  4.0 0.7 %copy-done.3 = s32[3,256]{1,0:T(4,128)S(1)} copy-done((s32[3,256]{1,0:T(4,128)S(1)}, s32[3,256]{1,0:T(4,128)}, u32[]{:S(2)}) %copy-start.3) | copy-done | bytes 3096
  4.7 0.0 copy-start.4
  4.7 0.7 %copy-done.4 = f32[4,256]{1,0:T(4,128)S(1)} copy-done((f32[4,256]{1,0:T(4,128)S(1)}, f32[4,256]{1,0:T(4,128)}, u32[]{:S(2)}) %copy-start.4) | copy-done | bytes 4120
  5.4 0.0 copy-start.5
  5.4 0.7 %copy-done.5 = s32[3,8]{1,0:T(4,128)S(1)} copy-done((s32[3,8]{1,0:T(4,128)S(1)}, s32[3,8]{1,0:T(4,128)}, u32[]{:S(2)}) %copy-start.5) | copy-done | bytes 120
  6.1 0.0 copy-start.6
  6.1 0.7 %copy-done.6 = f32[4,8]{1,0:T(4,128)S(1)} copy-done((f32[4,8]{1,0:T(4,128)S(1)}, f32[4,8]{1,0:T(4,128)}, u32[]{:S(2)}) %copy-start.6) | copy-done | bytes 152
  6.8 0.0 copy-start.7
  6.8 0.7 %copy-done.7 = s32[2,2]{1,0:T(2,128)S(1)} copy-done((s32[2,2]{1,0:T(2,128)S(1)}, s32[2,2]{1,0:T(2,128)}, u32[]{:S(2)}) %copy-start.7) | copy-done | bytes 40
  7.5 0.0 copy-start.8
  7.5 0.7 %copy-done.8 = s32[17]{0:T(128)S(1)} copy-done((s32[17]{0:T(128)S(1)}, s32[17]{0:T(128)}, u32[]{:S(2)}) %copy-start.8) | copy-done | bytes 92
  8.1 46.8 %shard_map.104 = (f32[32,48,128]{2,1,0:T(8,128)S(1)}, f32[2304,128]{1,0:T(8,128)S(1)}) custom-call(f32[32,48,128]{2,1,0:T(8,128)S(1)} %copy-done, f32[32,48,128]{2,1,0:T(8,128)S(1)} %copy-done.1, f32[32,48,128]{2,1,0:T(8,128)S(1)} %copy-done.2, s32[3,8]{1,0:T(4,128)S(1)} %copy-done.5, f32[4,8]{1,0:T(4,128)S(1)} %copy-done.6, s32[3,256]{1,0:T(4,128)S(1)} %copy-done.3, ...), custom_call_target="tpu_custom_call" | custom-call | tf_op jit(solution)/shard_map/pallas_call | solution.py:338
  54.9 0.5 copy.15
  55.5 1.1 %reshape.11 = f32[16,17,768]{2,0,1:T(8,128)} reshape(f32[16,17,6,128]{3,2,0,1:T(8,128)S(1)} %bitcast.8) | data formatting | bytes 1671168 | tf_op jit(solution)/shard_map/reshape | solution.py:372
  56.5 0.9 %copy.17 = f32[32,48,128]{2,1,0:T(8,128)} copy(f32[32,48,128]{2,1,0:T(8,128)S(1)} %get-tuple-element.8) | data formatting | bytes 1572864
Async XLA Ops:
  0.6 1.1 %copy-start = (f32[32,48,128]{2,1,0:T(8,128)S(1)}, f32[32,48,128]{2,1,0:T(8,128)}, u32[]{:S(2)}) copy-start(f32[32,48,128]{2,1,0:T(8,128)} %now_ref.1) | copy-start | bytes 2359300
  1.8 1.1 %copy-start.1 = (f32[32,48,128]{2,1,0:T(8,128)S(1)}, f32[32,48,128]{2,1,0:T(8,128)}, u32[]{:S(2)}) copy-start(f32[32,48,128]{2,1,0:T(8,128)} %prev_ref.1) | copy-start | bytes 2359300
  2.9 1.1 %copy-start.2 = (f32[32,48,128]{2,1,0:T(8,128)S(1)}, f32[32,48,128]{2,1,0:T(8,128)}, u32[]{:S(2)}) copy-start(f32[32,48,128]{2,1,0:T(8,128)} %courant_ref.1) | copy-start | bytes 2359300
  4.0 0.7 %copy-start.3 = (s32[3,256]{1,0:T(4,128)S(1)}, s32[3,256]{1,0:T(4,128)}, u32[]{:S(2)}) copy-start(s32[3,256]{1,0:T(4,128)} %rcell_ref.1) | copy-start | bytes 9220
  4.7 0.7 %copy-start.4 = (f32[4,256]{1,0:T(4,128)S(1)}, f32[4,256]{1,0:T(4,128)}, u32[]{:S(2)}) copy-start(f32[4,256]{1,0:T(4,128)} %rwave_ref.1) | copy-start | bytes 12292
  5.4 0.7 %copy-start.5 = (s32[3,8]{1,0:T(4,128)S(1)}, s32[3,8]{1,0:T(4,128)}, u32[]{:S(2)}) copy-start(s32[3,8]{1,0:T(4,128)} %scell_ref.1) | copy-start | bytes 292
  6.1 0.7 %copy-start.6 = (f32[4,8]{1,0:T(4,128)S(1)}, f32[4,8]{1,0:T(4,128)}, u32[]{:S(2)}) copy-start(f32[4,8]{1,0:T(4,128)} %swave_ref.1) | copy-start | bytes 388
  6.8 0.7 %copy-start.7 = (s32[2,2]{1,0:T(2,128)S(1)}, s32[2,2]{1,0:T(2,128)}, u32[]{:S(2)}) copy-start(s32[2,2]{1,0:T(2,128)} %steps_ref.1) | copy-start | bytes 52
  7.5 0.7 %copy-start.8 = (s32[17]{0:T(128)S(1)}, s32[17]{0:T(128)}, u32[]{:S(2)}) copy-start(s32[17]{0:T(128)} %lag_ref.1) | copy-start | bytes 208
where the time goes:
time: 57.8 us; the launch traced here: 57.4 us
  Pallas kernels  46.8 us (81%)
  local copies, waits for them, and re-layouts  9.93 us (17%)
  between operations  0.67 us (1%)
    pallas_call x1, Pallas kernels, body(): pl.pallas_call(kernel, out_shape=(jax.ShapeDtypeStruct(now.shape, f32), j...  46.8 us
    unnamed x20, local copies, waits for them, and re-layouts  8.84 us

commit v1 on v0

--- a/solution.py
+++ b/solution.py
@@ -24,9 +24,10 @@
 
 
 def kernel(
-    now_ref, prev_ref, courant_ref, scell_ref, swave_ref, rcell_ref, rwave_ref, steps_ref, lag_ref,
+    now_ref, prev_ref, courant_ref, scell_in, swave_in, rcell_in, rwave_in, steps_in, lag_in,
     final_ref, image_ref,
-    fields, courant, band, inject, choose_own, choose_other, snap, other, x_own, x_other, cells, waves,
+    scell_ref, swave_ref, rcell_ref, rwave_ref, steps_ref, lag_ref,
+    fields, courant, band, inject, choose_own, choose_other, snap, sent, other, x_own, x_other, total_ref, cells, waves,
     x_send, x_recv, y_send, y_recv, t_send, t_recv, local,
 ):
     nx, ny, nz = now_ref.shape
@@ -56,7 +57,14 @@
         pltpu.make_async_copy(prev_ref, fields.at[1, inner[0], inner[1]], local.at[1]),
         pltpu.make_async_copy(courant_ref, courant, local.at[2]),
     ]
-    for load in loads:
+    small = (
+        (scell_in, scell_ref), (swave_in, swave_ref), (rcell_in, rcell_ref),
+        (rwave_in, rwave_ref), (steps_in, steps_ref), (lag_in, lag_ref),
+    )
+    tables = [
+        pltpu.make_async_copy(src, dst, local.at[4 + i]) for i, (src, dst) in enumerate(small)
+    ]
+    for load in tables + loads:
         load.start()
 
     for parity in range(2):
@@ -118,7 +126,7 @@
 
     def trade(k):
         return pltpu.make_async_remote_copy(
-            src_ref=snap.at[k],
+            src_ref=sent.at[k],
             dst_ref=other.at[k],
             send_sem=t_send.at[k],
             recv_sem=t_recv.at[k],
@@ -168,6 +176,8 @@
     band[nz:2 * nz] = matrix_high
     band[2 * nz:] = matrix_low
 
+    for load in tables:
+        load.wait()
     is_source = which == 0
     count = scell_ref.shape[1]
     cells[...] = jnp.full(cells.shape, -1, jnp.int32)
@@ -202,22 +212,22 @@
     lax.fori_loop(0, nx // GROUP, spread, 0)
 
     quarter = nz // 4
+    middle = nz // 2
     lane = lax.broadcasted_iota(jnp.int32, (nz, nz), 1)
     depth = lax.broadcasted_iota(jnp.int32, (nz, nz), 0)
     twice = 2 * (which * quarter + lax.rem(lane, quarter)) - depth
     spot = lane // quarter
     sign = jnp.where(is_source, -1, 1)
     far = 4 * nz
-
-    def choose(h, carry):
-        lag = lag_ref[h] * sign
-        for r in range(4):
-            mine = jnp.where(spot == r, twice, far)
-            choose_own[h, r * nz:(r + 1) * nz, :] = jnp.where(mine == -lag, f32(1.0), f32(0.0)).astype(bf16)
-            choose_other[h, r * nz:(r + 1) * nz, :] = jnp.where(mine == lag, f32(1.0), f32(0.0)).astype(bf16)
-        return carry
-
-    lax.fori_loop(0, lags, choose, 0)
+    sets = -(-lags // 4)
+    for g in range(sets):
+        lag = jnp.full((nz, nz), far, jnp.int32)
+        for i in range(min(4, lags - 4 * g)):
+            lag = jnp.where(spot == i, lag_ref[4 * g + i] * sign, lag)
+        for ref, hit in ((choose_own, twice == -lag), (choose_other, twice == lag)):
+            one = jnp.where(hit, f32(1.0), f32(0.0)).astype(bf16)
+            ref[g, 0:nz, :] = one
+            ref[g, nz:, :] = one
 
     for load in loads:
         load.wait()
@@ -256,31 +266,80 @@
 
         lax.fori_loop(0, nx // 2, one, 0)
 
-    def split(ref, k, to):
-        count = ref.shape[2]
+    packed = snap.shape[2]
+    part_rows = packed // 4
+    edge_row = 2 * packed
+
+    def pack(k):
+        place = lax.broadcasted_iota(jnp.int32, (packed, nz), 1)
+        strip = lax.broadcasted_iota(jnp.int32, (part_rows, nz), 1) // ROW
+        for pair in range(2):
+            even, odd = snap[k, 2 * pair], snap[k, 2 * pair + 1]
+            first = jnp.where(is_source, pltpu.roll(even, middle, 1), even)
+            second = jnp.where(is_source, odd, pltpu.roll(odd, middle, 1))
+            sent[k, pair * packed:(pair + 1) * packed, :] = jnp.where(place < middle, first, second)
+        edge = jnp.zeros((part_rows, nz), f32)
         for r in range(4):
-            high, low = halves(ref[k, r])
-            to[0:count, r * nz:(r + 1) * nz] = high
-            to[count:, r * nz:(r + 1) * nz] = low
+            plane = snap[k, r]
+            plane = jnp.where(is_source, pltpu.roll(plane, ROW, 1), plane)
+            for j in range(4):
+                slot = 4 * r + j
+                piece = plane[j * part_rows:(j + 1) * part_rows]
+                by = (slot * ROW - middle) % nz
+                piece = pltpu.roll(piece, by, 1) if by else piece
+                edge = jnp.where(strip == slot, piece, edge)
+        sent[k, edge_row:, :] = edge
+
+    def unpack(k):
+        place = lax.broadcasted_iota(jnp.int32, (packed, nz), 1)
+        main = jnp.where(is_source, place, nz - 1 - place) < middle
+        from_edge = jnp.where(is_source, middle, middle - ROW)
+        near = (place >= from_edge) & (place < from_edge + ROW)
+        edge = other[k, edge_row:, :]
+        for r in range(4):
+            pair = r // 2
+            straight = other[k, pair * packed:(pair + 1) * packed, :]
+            turned = pltpu.roll(straight, middle, 1)
+            if r % 2 == 0:
+                body_part = jnp.where(is_source, straight, turned)
+            else:
+                body_part = jnp.where(is_source, turned, straight)
+            pieces = []
+            for j in range(4):
+                by = (middle - (4 * r + j) * ROW) % nz
+                pieces.append(pltpu.roll(edge, by, 1) if by else edge)
+            rim = jnp.concatenate(pieces, axis=0)
+            rim = jnp.where(is_source, rim, pltpu.roll(rim, nz - ROW, 1))
+            high, low = halves(jnp.where(main, body_part, jnp.where(near, rim, 0.0)))
+            x_other[r * packed:(r + 1) * packed, 0:nz] = high
+            x_other[r * packed:(r + 1) * packed, nz:] = low
 
     def image(k):
-        split(snap, k, x_own)
+        for r in range(4):
+            high, low = halves(snap[k, r])
+            x_own[r * packed:(r + 1) * packed, 0:nz] = high
+            x_own[r * packed:(r + 1) * packed, nz:] = low
         trade(k).wait_recv()
-        split(other, k, x_other)
-        count = snap.shape[2]
-
-        def one(h, carry):
-            mine = jnp.dot(x_own[...], choose_own[h], preferred_element_type=f32)
-            theirs = jnp.dot(x_other[...], choose_other[h], preferred_element_type=f32)
-            value = (mine[:count] + mine[count:]) * (theirs[:count] + theirs[count:])
-            place = pl.ds(h, count, image_ref.shape[0] // count)
+        unpack(k)
+        field_of = lax.broadcasted_iota(jnp.int32, (packed, nz), 1) // quarter
+        for g in range(sets):
+            mine = jnp.dot(x_own[...], choose_own[g], preferred_element_type=f32)
+            theirs = jnp.dot(x_other[...], choose_other[g], preferred_element_type=f32)
             if k == 0:
-                image_ref[place, :] = value
-            else:
-                image_ref[place, :] = image_ref[place, :] + value
-            return carry
-
-        lax.fori_loop(0, lags, one, 0)
+                total_ref[g] = mine * theirs
+                continue
+            value = total_ref[g] + mine * theirs
+            turned = []
+            for r in range(4):
+                piece = value[r * packed:(r + 1) * packed]
+                turned.append(pltpu.roll(piece, r * quarter, 1) if r else piece)
+            for i in range(min(4, lags - 4 * g)):
+                line = turned[0]
+                for r in range(1, 4):
+                    line = jnp.where(field_of == (i + r) % 4, turned[r], line)
+                line = pltpu.roll(line, nz - i * quarter, 1) if i else line
+                for q in range(ny // ROW):
+                    image_ref[4 * g + i, :, q * nz:(q + 1) * nz] = line[q * (nx // 2):(q + 1) * (nx // 2)]
 
     groups = nx // GROUP
     for s in range(1, STEPS + 1):
@@ -312,6 +371,7 @@
         if s % 2 == 0:
             k = s // 2 - 1
             hold(k, steps_ref[which, k])
+            pack(k)
             trade(k).start()
     store = pltpu.make_async_copy(fields.at[STEPS % 2, inner[0], inner[1]], final_ref, local.at[3])
     store.start()
@@ -328,32 +388,38 @@
 def body(now, prev, courant, source_cells, source_wave, receiver_cells, receiver_wave, steps, lag_offsets):
     nx, ny, nz = now.shape
     lags = lag_offsets.shape[0]
-    deep = -(-lags // 8) * 8
     packed = (nx // 2) * (ny // 8)
     points = receiver_cells.shape[1]
     vmem = pl.BlockSpec(memory_space=pltpu.VMEM)
-    smem = pl.BlockSpec(memory_space=pltpu.SMEM)
-    anywhere = pl.BlockSpec(memory_space=pl.ANY)
+    hbm = pl.BlockSpec(memory_space=pltpu.HBM)
     dma = pltpu.SemaphoreType.DMA
     final, image = pl.pallas_call(
         kernel,
         out_shape=(
             jax.ShapeDtypeStruct(now.shape, f32),
-            jax.ShapeDtypeStruct((packed * deep, nz), f32),
+            jax.ShapeDtypeStruct((lags, nx // 2, (ny // 8) * nz), f32),
         ),
-        in_specs=[anywhere] * 3 + [vmem] * 4 + [smem] * 2,
-        out_specs=(anywhere, vmem),
+        in_specs=[hbm] * 9,
+        out_specs=(hbm, vmem),
         scratch_shapes=[
+            pltpu.VMEM(source_cells.shape, jnp.int32),
+            pltpu.VMEM(source_wave.shape, f32),
+            pltpu.VMEM(receiver_cells.shape, jnp.int32),
+            pltpu.VMEM(receiver_wave.shape, f32),
+            pltpu.SMEM(steps.shape, jnp.int32),
+            pltpu.SMEM(lag_offsets.shape, jnp.int32),
             pltpu.VMEM((2, nx + 2 * WIDTH, ny + 2 * ROW, nz), f32),
             pltpu.VMEM((nx, ny, nz), f32),
             pltpu.VMEM((3 * nz, nz), bf16),
             pltpu.VMEM((STEPS, nx * ny, nz), f32),
-            pltpu.VMEM((lags, 4 * nz, nz), bf16),
-            pltpu.VMEM((lags, 4 * nz, nz), bf16),
+            pltpu.VMEM((-(-lags // 4), 2 * nz, nz), bf16),
+            pltpu.VMEM((-(-lags // 4), 2 * nz, nz), bf16),
             pltpu.VMEM((2, 4, packed, nz), f32),
-            pltpu.VMEM((2, 4, packed, nz), f32),
-            pltpu.VMEM((2 * packed, 4 * nz), bf16),
-            pltpu.VMEM((2 * packed, 4 * nz), bf16),
+            pltpu.VMEM((2, 2 * packed + packed // 4, nz), f32),
+            pltpu.VMEM((2, 2 * packed + packed // 4, nz), f32),
+            pltpu.VMEM((4 * packed, 2 * nz), bf16),
+            pltpu.VMEM((4 * packed, 2 * nz), bf16),
+            pltpu.VMEM((-(-lags // 4), 4 * packed, nz), f32),
             pltpu.VMEM((8, points), jnp.int32),
             pltpu.VMEM((8, points), f32),
             dma((STEPS, 2)),
@@ -362,15 +428,13 @@
             dma((STEPS, 3)),
             dma((2,)),
             dma((2,)),
-            dma((4,)),
+            dma((10,)),
         ],
         compiler_params=pltpu.CompilerParams(
-            collective_id=0, has_side_effects=True, vmem_limit_bytes=48 * 1024 * 1024
+            collective_id=0, has_side_effects=True, vmem_limit_bytes=62 * 1024 * 1024
         ),
     )(now, prev, courant, source_cells, source_wave, receiver_cells, receiver_wave, steps, lag_offsets)
-    image = image.reshape(ny // 8, nx // 2, deep, nz)[:, :, :lags]
-    image = jnp.transpose(image, (1, 2, 0, 3)).reshape(nx // 2, lags, (ny // 8) * nz)
-    return final, image
+    return final, jnp.transpose(image, (1, 0, 2))
 
 
 def solution(mesh):

time: 57.8 us -> 39.7 us (0.69)
  Pallas kernels: 46.8 us -> 35.8 us
  local copies, waits for them, and re-layouts: 9.93 us -> 3.04 us
    pallas_call x1, Pallas kernels: 46.8 us -> 35.8 us  [body(): pl.pallas_call(kernel, out_shape=(jax.ShapeDtypeStruct(now.shape, f32), j...]
    unnamed x20 -> x4, local copies, waits for them, and re-layouts: 8.84 us -> 3.04 us
    reshape x1 -> x0, local copies, waits for them, and re-layouts: 1.09 us -> none  [body(): jnp.transpose(image, (1, 2, 0, 3)).reshape(nx // 2, lags, ny // 8 * nz)]
where the time goes in v1:
time: 39.7 us; the launch traced here: 39.5 us
  Pallas kernels  35.8 us (90%)
  local copies, waits for them, and re-layouts  3.04 us (8%)
  between operations  0.65 us (2%)
    pallas_call x1, Pallas kernels, body(): pl.pallas_call(kernel, out_shape=(jax.ShapeDtypeStruct(now.shape, f32), j...  35.8 us
    unnamed x4, local copies, waits for them, and re-layouts  3.04 us

profile of v1, /device:TPU:0, one launch (start us, length us, event | category | flops | bytes accessed | tf_op | source)
XLA Modules:
  0.0 39.5 jit_solution(1285775434133504854)
XLA Ops:
  0.6 35.8 %shard_map.104 = (f32[32,48,128]{2,1,0:T(8,128)}, f32[17,16,768]{2,1,0:T(8,128)}) custom-call(f32[32,48,128]{2,1,0:T(8,128)} %now_ref.1, f32[32,48,128]{2,1,0:T(8,128)} %prev_ref.1, f32[32,48,128]{2,1,0:T(8,128)} %courant_ref.1, s32[3,8]{1,0:T(4,128)} %scell_in.1, f32[4,8]{1,0:T(4,128)} %swave_in.1, s32[3,256]{1,0:T(4,128)} %rcell_in.1, f32[4,256]{1,0:T(4,128)} %rwave_in.1, ...), custom_call_target="tpu_custom_call" | custom-call | tf_op jit(solution)/shard_map/pallas_call | solution.py:396
  36.5 0.0 copy-start
  36.5 2.1 %copy.13 = f32[32,48,128]{2,1,0:T(8,128)} copy(f32[32,48,128]{2,1,0:T(8,128)} %get-tuple-element.8) | data formatting | bytes 1572864
  38.6 0.0 copy-done
  38.6 0.9 %copy.14 = f32[16,17,768]{2,0,1:T(8,128)} copy(f32[16,17,768]{2,0,1:T(8,128)S(1)} %bitcast.1) | data formatting | bytes 1671168
Async XLA Ops:
  36.5 2.2 %copy-start = (f32[17,16,768]{2,1,0:T(8,128)S(1)}, f32[17,16,768]{2,1,0:T(8,128)}, u32[]{:S(2)}) copy-start(f32[17,16,768]{2,1,0:T(8,128)} %get-tuple-element.5) | copy-start | bytes 2506756
